TPU v7x, 32 devices: a whole 2x2x4 slice. The times are simulated.
32 devices in a mesh: row: 4 (over y, x), col: 8 (over z, core).
Axes of the slice: x: 2, y: 2, z: 4, core: 2. Of those that a mesh axis runs over, the one named last changes fastest.
Arguments:
- grad_out: bfloat16 [4096, 512], P(('row', 'col'))
- relu_mask: int32 [4096, 512], P(('row', 'col')), may hold values 0 or 1
- aggregated: bfloat16 [4096, 512], P(('row', 'col')), may hold values from -6 to 6
- weight: bfloat16 [512, 512], replicated, may hold values from -0.25 to 0.25
- adj_blocks: bfloat16 [4, 8, 5, 128, 128], P('row', 'col'), may hold values from 0 to 0.11867817
- block_pos: int32 [4, 8, 5], P('row', 'col'), may hold values from 0 to 31, as said below
- block_live: int32 [4, 8], P('row', 'col'), may hold values from 1 to 5, as said below
Outputs:
- grad_input: bfloat16 [8, 512, 512], P('col', 'row')
- grad_weight: float32 [512, 512], replicated
- grad_bias: float32 [512], replicated
Inputs may be any that keep to these rules, and one draw needn't show every extreme that they name: `block_pos`: within one tile the 5 slots name different positions; position p is block row p // 4, block column p % 4. `block_live`: some tile uses all 5 slots.
All inputs are finite; a program needn't handle non-finite values. No bound on the sum of `relu_mask` on one device may be relied on, other than what follows from the above.
Results may differ from a plain program's by a relative error of at most 0.005.
Values may be sent and summed in bfloat16 or wider, within the bound.
A program may use at most 64 MiB of HBM per device.

v0:
```python
import functools
import math

import jax
import jax.numpy as jnp
from jax import lax
from jax.experimental import pallas as pl
from jax.experimental.pallas import tpu as pltpu
from jax.sharding import PartitionSpec as P

MESH = pl.DeviceIdType.MESH
BF = jnp.bfloat16
F32 = jnp.float32
TILE = 16


def dot0(a, b):
    return lax.dot_general(a, b, (((0,), (0,)), ((), ())), preferred_element_type=F32)


def kernel(cfg, go_ref, mask_ref, agg_ref, w_ref, blk_ref, pos_ref, live_ref,
           gi_ref, gw_ref, gb_ref, *scr):
    n_row, n_col, nch, cap, group, scatter = cfg
    n_z = n_col // 2
    gath = scr[:nch]
    lhs, cbuf, rbuf, asib, gpart, grecv, zsend, zrecv, gw, go_v, mask_v, agg_v, w_v, blk_v, bsend, brecv = scr[nch:nch + 16]
    (ag_s, ag_r, fw_s, fw_r, c_s, c_r, as_s, as_r, g_s, g_r, z_s, z_r, wz_s, wz_r, wr_s, wr_r, wf_s, wf_r,
     b_s, b_r, in_s, sb_s, sb_r) = scr[nch + 16:]
    rows, feat = go_ref.shape
    fc = feat // nch
    blk = blk_ref.shape[-1]
    tbc = n_row * rows // blk
    half = feat // 2
    piece = half // n_row
    part = piece // n_z if scatter else piece
    me_r, me_c = lax.axis_index("row"), lax.axis_index("col")
    z, core = me_c // 2, me_c % 2
    sib = z * 2 + 1 - core
    sib_id = (me_r, sib)

    def row_id(d):
        return ((me_r + d) % n_row, me_c)

    def z_id(d):
        return (me_r, ((z + d) % n_z) * 2 + core)

    other = pl.ds(pl.multiple_of((1 - core) * half, half), half)
    mine = pl.ds(pl.multiple_of(core * half, half), half)
    loads = [pltpu.make_async_copy(src, dst, in_s.at[i]) for i, (src, dst) in enumerate((
        (go_ref, go_v), (mask_ref, mask_v), (agg_ref.at[:, mine], agg_v), (blk_ref.at[0, 0], blk_v), (w_ref, w_v)))]
    for c in loads:
        c.start()

    sent = []

    def copy(src, dst, s, r, dev):
        return pltpu.make_async_remote_copy(src_ref=src, dst_ref=dst, send_sem=s, recv_sem=r,
                                               device_id=dev, device_id_type=MESH)

    def send(*what):
        c = copy(*what)
        c.start()
        sent.append((None, lambda: copy(*what)))
        return c

    def send_when(now, make):
        pl.when(now)(lambda: make().start())
        sent.append((now, make))

    barrier = pltpu.get_barrier_semaphore()
    peers = [sib_id] + [z_id(d) for d in range(1, n_z)] + [row_id(d) for d in range(1, n_row)]
    for p in peers:
        pl.semaphore_signal(barrier, inc=1, device_id=p, device_id_type=MESH)

    loads[0].wait()
    loads[1].wait()
    for ch in range(nch):
        cols = slice(ch * fc, (ch + 1) * fc)
        gath[ch][me_c] = go_v[:, cols] * mask_v[:, cols].astype(F32).astype(BF)

    pl.semaphore_wait(barrier, len(peers))

    has_next = (z < n_z - 1, z > 0)
    next_id = ((me_r, me_c + 2), (me_r, me_c - 2))
    sib_cp = []
    agg_cp = send(agg_ref.at[:, other], asib, as_s, as_r, sib_id)
    for ch in range(nch):
        own = gath[ch].at[me_c]
        sib_cp.append(send(own, own, sb_s.at[ch], sb_r.at[ch], sib_id))

    def depart(ch):
        own = gath[ch].at[me_c]
        for way in range(2):
            send_when(has_next[way], lambda way=way: copy(
                own, own, ag_s.at[ch, way, 0], ag_r.at[ch, way, 0], next_id[way]))

    depart(0)

    loads[2].wait()
    agg_cp.wait_recv()
    for ch in range(nch):
        cols = slice(ch * fc, (ch + 1) * fc)
        sib_cp[ch].wait_recv()
        g = dot0(agg_v[...], gath[ch][me_c]) + dot0(asib[...], gath[ch][sib])
        gpart[:, :, cols] = g.astype(BF).reshape(n_row, piece, fc)
    g_cp = [send(gpart.at[(me_r + d) % n_row], grecv.at[d - 1], g_s.at[d - 1], g_r.at[d - 1], row_id(d))
            for d in range(1, n_row)]

    def arrival(way, step):
        src = z - 1 - step if way == 0 else z + 1 + step
        return src, (src >= 0 if way == 0 else src <= n_z - 1)

    def relay(ch, step):
        for way in range(2):
            src, there = arrival(way, step)

            slot = gath[ch].at[src * 2 + core]
            on = there & has_next[way]

            def hop(step, way=way, slot=slot):
                return copy(slot, slot, ag_s.at[ch, way, step], ag_r.at[ch, way, step], next_id[way])

            def over(way=way, slot=slot):
                return copy(slot, slot, fw_s.at[ch, way, step], fw_r.at[ch, way, step], sib_id)

            pl.when(there)(lambda hop=hop: hop(step).wait_recv())
            if step + 1 < n_z - 1:
                send_when(on, functools.partial(hop, step + 1))
            send_when(there, over)

    def gathered(ch):
        for step in range(n_z - 1):
            for way in range(2):
                src, there = arrival(way, step)

                def come(way=way, step=step, src=src):
                    slot = gath[ch].at[src * 2 + 1 - core]
                    copy(slot, slot, fw_s.at[ch, way, step], fw_r.at[ch, way, step], sib_id).wait_recv()

                pl.when(there)(come)

    def contribute(ch):
        gathered(ch)
        if cap == group:
            rhs = jnp.concatenate([gath[ch][pos_ref[0, 0, k] // tbc] for k in range(cap)], axis=0)
            cbuf[ch] = jnp.dot(lhs[...], rhs, preferred_element_type=F32).astype(BF).reshape(n_row, rows, fc)
        else:
            acc_ref = lhs
            acc_ref[...] = jnp.zeros_like(acc_ref)

            def turn(t, carry):
                for i in range(group):
                    k = t * group + i
                    p = pos_ref[0, 0, k]
                    rhs = gath[ch][p // tbc]
                    prod = dot0(blk_v[k], rhs)
                    alive = k < live_ref[0, 0]
                    for j in range(tbc):
                        acc_ref[j * blk:(j + 1) * blk] += jnp.where(alive & (p % tbc == j), prod, 0.0)
                return carry

            lax.fori_loop(0, cap // group, turn, 0)
            cbuf[ch] = acc_ref[...].astype(BF).reshape(n_row, rows, fc)
        return [send(cbuf.at[ch, (me_r + d) % n_row], rbuf.at[ch, d - 1], c_s.at[ch, d - 1], c_r.at[ch, d - 1], row_id(d))
                for d in range(1, n_row)]

    total = None

    def project(ch, cps):
        for c in cps:
            c.wait_recv()
        s = cbuf[ch, me_r].astype(F32)
        for d in range(1, n_row):
            s += rbuf[ch, d - 1].astype(F32)
        return lax.dot_general(s.astype(BF), w_v[:, ch * fc:(ch + 1) * fc], (((1,), (1,)), ((), ())),
                               preferred_element_type=F32)

    base = core * half
    at_row = pl.ds(pl.multiple_of(base + me_r * piece, piece), piece)
    at_me = pl.ds(pl.multiple_of(base + me_r * piece + (z * part if scatter else 0), part), part)

    relay(0, 0)
    for ch in range(1, nch):
        depart(ch)

    loads[3].wait()
    if cap == group:
        for k in range(cap):
            at = pos_ref[0, 0, k] % tbc
            alive = k < live_ref[0, 0]
            turned = blk_v[k].T
            for j in range(tbc):
                lhs[j * blk:(j + 1) * blk, k * blk:(k + 1) * blk] = jnp.where(
                    alive & (at == j), turned, jnp.zeros((blk, blk), BF))

    for step in range(1, n_z - 2):
        relay(0, step)
    for c in g_cp:
        c.wait_recv()
    acc = gpart[me_r].astype(F32)
    for d in range(1, n_row):
        acc += grecv[d - 1].astype(F32)
    zsend[...] = acc.astype(BF).reshape(zsend.shape)
    zpick = [zsend.at[(z + d) % n_z if scatter else 0] for d in range(n_z)]
    zz_cp = [send(zpick[d], zrecv.at[d - 1], z_s.at[d - 1], z_r.at[d - 1], z_id(d)) for d in range(1, n_z)]

    def z_sum():
        for c in zz_cp:
            c.wait_recv()
        acc = zpick[0][...].astype(F32)
        for d in range(1, n_z):
            acc += zrecv[d - 1].astype(F32)
        gw[at_me] = acc.astype(BF)
        if not scatter:
            return []
        return [send(gw.at[at_me], gw.at[at_me], wz_s.at[d - 1], wz_r.at[d - 1], z_id(d)) for d in range(1, n_z)]

    lanes = 128
    if n_z > 2:
        relay(0, n_z - 2)
    for ch in range(1, nch):
        relay(ch, 0)
    c_cp = [contribute(0)]
    wz_cp = z_sum()
    for step in range(1, n_z - 1):
        for ch in range(1, nch):
            relay(ch, step)
    for c in wz_cp:
        c.wait_recv()
    wr_cp = [send(gw.at[at_row], gw.at[at_row], wr_s.at[d - 1], wr_r.at[d - 1], row_id(d)) for d in range(1, n_row)]
    wf_cp = [send(gw.at[at_row], gw.at[at_row], wf_s.at[0], wf_r.at[0], sib_id)]
    for ch in range(1, nch):
        c_cp.append(contribute(ch))

    bsend[...] = jnp.zeros_like(bsend)
    ones = jnp.ones((TILE, n_col * rows), BF)
    for ch in range(nch):
        sums = lax.dot_general(ones, gath[ch][...].reshape(n_col * rows, fc), (((1,), (0,)), ((), ())),
                               preferred_element_type=F32)
        for i in range(fc // lanes):
            at = ch * (fc // lanes) + i
            bsend[at:at + 1, :] = sums[0:1, i * lanes:(i + 1) * lanes]
    b_cp = [send(bsend, brecv.at[d - 1], b_s.at[d - 1], b_r.at[d - 1], row_id(d)) for d in range(1, n_row)]

    loads[4].wait()
    for ch in range(nch - 1):
        more = project(ch, c_cp[ch])
        total = more if total is None else total + more
    for d in range(1, n_row):
        wr_cp[d - 1].wait_recv()
        src = pl.ds(pl.multiple_of(base + ((me_r + n_row - d) % n_row) * piece, piece), piece)
        wf_cp.append(send(gw.at[src], gw.at[src], wf_s.at[d], wf_r.at[d], sib_id))
    gw_ref[mine] = gw[mine]
    more = project(nch - 1, c_cp[nch - 1])
    total = more if total is None else total + more
    gi_ref[...] = total.astype(BF)
    bias = bsend[...]
    for d in range(1, n_row):
        b_cp[d - 1].wait_recv()
        bias += brecv[d - 1]
    gb_ref[...] = bias
    for c in wf_cp:
        c.wait_recv()
    gw_ref[other] = gw[other]
    for now, make in sent:
        if now is None:
            make().wait_send()
        else:
            pl.when(now)(lambda make=make: make().wait_send())


def body(n_row, n_col, grad_out, relu_mask, aggregated, weight, adj_blocks, block_pos, block_live):
    rows, feat = grad_out.shape
    cap, blk = adj_blocks.shape[2], adj_blocks.shape[-1]
    group = max(d for d in range(1, 17) if cap % d == 0)
    nch = 2
    fc = feat // nch
    n_z = n_col // 2
    piece = feat // 2 // n_row
    scatter = piece % (n_z * TILE) == 0
    part = piece // n_z if scatter else piece
    tbc = n_row * rows // blk
    brows = -(-feat // 1024) * 8
    if cap == group:
        lhs = pltpu.VMEM((tbc * blk, cap * blk), BF)
    else:
        lhs = pltpu.VMEM((tbc * blk, fc), F32)
    dma = pltpu.SemaphoreType.DMA
    scratch = [pltpu.VMEM((n_col, rows, fc), BF) for _ in range(nch)] + [
        lhs,
        pltpu.VMEM((nch, n_row, rows, fc), BF),
        pltpu.VMEM((nch, n_row - 1, rows, fc), BF),
        pltpu.VMEM((rows, feat // 2), BF),
        pltpu.VMEM((n_row, piece, feat), BF),
        pltpu.VMEM((n_row - 1, piece, feat), BF),
        pltpu.VMEM((n_z if scatter else 1, part, feat), BF),
        pltpu.VMEM((n_z - 1, part, feat), BF),
        pltpu.VMEM((feat, feat), BF),
        pltpu.VMEM((rows, feat), BF),
        pltpu.VMEM((rows, feat), jnp.int32),
        pltpu.VMEM((rows, feat // 2), BF),
        pltpu.VMEM((feat, feat), BF),
        pltpu.VMEM((cap, blk, blk), BF),
        pltpu.VMEM((brows, 128), F32),
        pltpu.VMEM((n_row - 1, brows, 128), F32),
    ]
    sems = [dma((nch, 2, n_z - 1)), dma((nch, 2, n_z - 1)), dma((nch, 2, n_z - 1)), dma((nch, 2, n_z - 1)),
            dma((nch, n_row - 1)), dma((nch, n_row - 1)), dma(()), dma(()),
            dma((n_row - 1,)), dma((n_row - 1,)), dma((n_z - 1,)), dma((n_z - 1,)),
            dma((n_z - 1,)), dma((n_z - 1,)), dma((n_row - 1,)), dma((n_row - 1,)),
            dma((n_row,)), dma((n_row,)), dma((n_row - 1,)), dma((n_row - 1,)), dma((5,)),
            dma((nch,)), dma((nch,))]
    vm = pl.BlockSpec(memory_space=pltpu.VMEM)
    hbm = pl.BlockSpec(memory_space=pltpu.HBM)
    sm = pl.BlockSpec(memory_space=pltpu.SMEM)
    gi, gw, gb = pl.pallas_call(
        functools.partial(kernel, (n_row, n_col, nch, cap, group, scatter)),
        out_shape=(jax.ShapeDtypeStruct((rows, feat), BF),
                   jax.ShapeDtypeStruct((feat, feat), BF),
                   jax.ShapeDtypeStruct((brows, 128), F32)),
        in_specs=[hbm, hbm, hbm, hbm, hbm, sm, sm],
        out_specs=(vm, vm, vm),
        scratch_shapes=scratch + sems,
        compiler_params=pltpu.CompilerParams(collective_id=0, has_side_effects=True,
                                             vmem_limit_bytes=(8 if cap == group else 48) * 1024 * 1024),
    )(*(pltpu.with_memory_space_constraint(x, pltpu.HBM)
        for x in (grad_out, relu_mask, aggregated, weight, adj_blocks)), block_pos, block_live)
    factor = 1.0 / math.sqrt(rows * n_row * n_col)
    return gi.reshape(1, rows, feat), gw.astype(F32) * factor, gb.reshape(-1)[:feat] * factor


def solution(mesh):
    return jax.shard_map(
        functools.partial(body, mesh.shape["row"], mesh.shape["col"]),
        mesh=mesh,
        in_specs=(
            P(("row", "col"), None),
            P(("row", "col"), None),
            P(("row", "col"), None),
            P(),
            P("row", "col", None, None, None),
            P("row", "col", None),
            P("row", "col"),
        ),
        out_specs=(P("col", "row", None), P(), P()),
        check_vma=False,
    )
```

profile of v0, /device:TPU:0, one launch (start us, length us, event | category | flops | bytes accessed | tf_op | source)
XLA Modules:
  0.0 34.3 jit_solution(2297898700556315519)
XLA Ops:
  0.6 0.0 copy-start
  1.3 0.0 copy-done
  1.3 30.7 %shard_map.94 = (bf16[128,512]{1,0:T(8,128)(2,1)S(1)}, bf16[512,512]{1,0:T(8,128)(2,1)S(1)}, f32[8,128]{1,0:T(8,128)S(1)}) custom-call(bf16[128,512]{1,0:T(8,128)(2,1)} %go_ref.1, s32[128,512]{1,0:T(8,128)} %mask_ref.1, bf16[128,512]{1,0:T(8,128)(2,1)} %agg_ref.1, bf16[512,512]{1,0:T(8,128)(2,1)} %w_ref.1, bf16[1,1,5,128,128]{4,3,2,1,0:T(8,128)(2,1)} %blk_ref.1, ...), custom_call_target="tpu_custom_call" | custom-call | tf_op jit(solution)/shard_map/pallas_call | solution.py:316
  32.0 0.6 %multiply_bitcast_fusion = f32[512]{0:T(512)} fusion(f32[8,128]{1,0:T(8,128)S(1)} %get-tuple-element.8), kind=kLoop, calls=%fused_computation.1 | loop fusion | flops 512 | bytes 4096 | tf_op jit(solution)/shard_map/mul | solution.py:329
  32.6 1.1 %convert_multiply_fusion = f32[512,512]{1,0:T(8,128)} fusion(bf16[512,512]{1,0:T(8,128)(2,1)S(1)} %get-tuple-element.7), kind=kLoop, calls=%fused_computation | loop fusion | flops 524288 | bytes 1572864 | tf_op jit(solution)/shard_map/mul | solution.py:329
  33.7 0.7 %copy.12 = bf16[1,128,512]{2,1,0:T(8,128)(2,1)} copy(bf16[1,128,512]{2,1,0:T(8,128)(2,1)S(1)} %bitcast.3) | data formatting | bytes 262144
Async XLA Ops:
  0.6 0.7 %copy-start = (s32[1,1,5]{2,1,0:T(1,128)S(1)}, s32[1,1,5]{2,1,0:T(1,128)}, u32[]{:S(2)}) copy-start(s32[1,1,5]{2,1,0:T(1,128)} %pos_ref.1) | copy-start | bytes 64
where the time goes:
time: 34.5 us; the launch traced here: 34.3 us
  Pallas kernels  30.7 us (89%)
  other arithmetic  1.69 us (5%)
  between operations  1.32 us (4%)
  local copies, waits for them, and re-layouts  0.66 us (2%)
    pallas_call x1, Pallas kernels, body(): pl.pallas_call(functools.partial(kernel, (n_row, n_col, nch, cap, group,...  30.7 us
    mul x1, other arithmetic, body(): gw.astype(F32) * factor  1.11 us

commit v1 on v0

--- a/solution.py
+++ b/solution.py
@@ -94,7 +94,8 @@
             send_when(has_next[way], lambda way=way: copy(
                 own, own, ag_s.at[ch, way, 0], ag_r.at[ch, way, 0], next_id[way]))
 
-    depart(0)
+    for ch in range(2):
+        depart(ch)
 
     loads[2].wait()
     agg_cp.wait_recv()
@@ -138,6 +139,10 @@
                     copy(slot, slot, fw_s.at[ch, way, step], fw_r.at[ch, way, step], sib_id).wait_recv()
 
                 pl.when(there)(come)
+
+    lanes = 128
+    ones = jnp.ones((TILE, n_col * rows), BF)
+    bsend[...] = jnp.zeros_like(bsend)
 
     def contribute(ch):
         gathered(ch)
@@ -161,8 +166,14 @@
 
             lax.fori_loop(0, cap // group, turn, 0)
             cbuf[ch] = acc_ref[...].astype(BF).reshape(n_row, rows, fc)
-        return [send(cbuf.at[ch, (me_r + d) % n_row], rbuf.at[ch, d - 1], c_s.at[ch, d - 1], c_r.at[ch, d - 1], row_id(d))
-                for d in range(1, n_row)]
+        cps = [send(cbuf.at[ch, (me_r + d) % n_row], rbuf.at[ch, d - 1], c_s.at[ch, d - 1], c_r.at[ch, d - 1], row_id(d))
+               for d in range(1, n_row)]
+        sums = lax.dot_general(ones, gath[ch][...].reshape(n_col * rows, fc), (((1,), (0,)), ((), ())),
+                               preferred_element_type=F32)
+        for i in range(fc // lanes):
+            at = ch * (fc // lanes) + i
+            bsend[at:at + 1, :] = sums[0:1, i * lanes:(i + 1) * lanes]
+        return cps
 
     total = None
 
@@ -179,30 +190,29 @@
     at_row = pl.ds(pl.multiple_of(base + me_r * piece, piece), piece)
     at_me = pl.ds(pl.multiple_of(base + me_r * piece + (z * part if scatter else 0), part), part)
 
-    relay(0, 0)
-    for ch in range(1, nch):
-        depart(ch)
-
-    loads[3].wait()
-    if cap == group:
-        for k in range(cap):
-            at = pos_ref[0, 0, k] % tbc
-            alive = k < live_ref[0, 0]
-            turned = blk_v[k].T
-            for j in range(tbc):
-                lhs[j * blk:(j + 1) * blk, k * blk:(k + 1) * blk] = jnp.where(
-                    alive & (at == j), turned, jnp.zeros((blk, blk), BF))
-
-    for step in range(1, n_z - 2):
-        relay(0, step)
-    for c in g_cp:
-        c.wait_recv()
-    acc = gpart[me_r].astype(F32)
-    for d in range(1, n_row):
-        acc += grecv[d - 1].astype(F32)
-    zsend[...] = acc.astype(BF).reshape(zsend.shape)
+    def spread():
+        loads[3].wait()
+        if cap == group:
+            for k in range(cap):
+                at = pos_ref[0, 0, k] % tbc
+                alive = k < live_ref[0, 0]
+                turned = blk_v[k].T
+                for j in range(tbc):
+                    lhs[j * blk:(j + 1) * blk, k * blk:(k + 1) * blk] = jnp.where(
+                        alive & (at == j), turned, jnp.zeros((blk, blk), BF))
+
     zpick = [zsend.at[(z + d) % n_z if scatter else 0] for d in range(n_z)]
-    zz_cp = [send(zpick[d], zrecv.at[d - 1], z_s.at[d - 1], z_r.at[d - 1], z_id(d)) for d in range(1, n_z)]
+    zz_cp, wz_cp, wr_cp, wf_cp = [], [], [], []
+
+    def row_sum():
+        for c in g_cp:
+            c.wait_recv()
+        acc = gpart[me_r].astype(F32)
+        for d in range(1, n_row):
+            acc += grecv[d - 1].astype(F32)
+        zsend[...] = acc.astype(BF).reshape(zsend.shape)
+        for d in range(1, n_z):
+            zz_cp.append(send(zpick[d], zrecv.at[d - 1], z_s.at[d - 1], z_r.at[d - 1], z_id(d)))
 
     def z_sum():
         for c in zz_cp:
@@ -211,39 +221,34 @@
         for d in range(1, n_z):
             acc += zrecv[d - 1].astype(F32)
         gw[at_me] = acc.astype(BF)
-        if not scatter:
-            return []
-        return [send(gw.at[at_me], gw.at[at_me], wz_s.at[d - 1], wz_r.at[d - 1], z_id(d)) for d in range(1, n_z)]
-
-    lanes = 128
-    if n_z > 2:
-        relay(0, n_z - 2)
-    for ch in range(1, nch):
-        relay(ch, 0)
-    c_cp = [contribute(0)]
-    wz_cp = z_sum()
-    for step in range(1, n_z - 1):
-        for ch in range(1, nch):
-            relay(ch, step)
-    for c in wz_cp:
-        c.wait_recv()
-    wr_cp = [send(gw.at[at_row], gw.at[at_row], wr_s.at[d - 1], wr_r.at[d - 1], row_id(d)) for d in range(1, n_row)]
-    wf_cp = [send(gw.at[at_row], gw.at[at_row], wf_s.at[0], wf_r.at[0], sib_id)]
-    for ch in range(1, nch):
-        c_cp.append(contribute(ch))
-
-    bsend[...] = jnp.zeros_like(bsend)
-    ones = jnp.ones((TILE, n_col * rows), BF)
+        if scatter:
+            for d in range(1, n_z):
+                wz_cp.append(send(gw.at[at_me], gw.at[at_me], wz_s.at[d - 1], wz_r.at[d - 1], z_id(d)))
+
+    def row_gather():
+        for c in wz_cp:
+            c.wait_recv()
+        for d in range(1, n_row):
+            wr_cp.append(send(gw.at[at_row], gw.at[at_row], wr_s.at[d - 1], wr_r.at[d - 1], row_id(d)))
+        wf_cp.append(send(gw.at[at_row], gw.at[at_row], wf_s.at[0], wf_r.at[0], sib_id))
+
+    c_cp = []
+    todo = []
     for ch in range(nch):
-        sums = lax.dot_general(ones, gath[ch][...].reshape(n_col * rows, fc), (((1,), (0,)), ((), ())),
-                               preferred_element_type=F32)
-        for i in range(fc // lanes):
-            at = ch * (fc // lanes) + i
-            bsend[at:at + 1, :] = sums[0:1, i * lanes:(i + 1) * lanes]
+        at = 1.9 * (ch // 2) + 0.1 * ch
+        if ch >= 2:
+            todo.append((at - 1.6 + 0.8 * (ch % 2), functools.partial(depart, ch)))
+        for step in range(n_z - 1):
+            todo.append((at + step, functools.partial(relay, ch, step)))
+        todo.append((at + n_z - 2 + 0.85, lambda ch=ch: c_cp.append(contribute(ch))))
+    todo += [(0.7, spread), (1.6, row_sum), (n_z - 0.91, z_sum), (n_z + 0.6, row_gather)]
+    for _, act in sorted(todo, key=lambda item: item[0]):
+        act()
+
     b_cp = [send(bsend, brecv.at[d - 1], b_s.at[d - 1], b_r.at[d - 1], row_id(d)) for d in range(1, n_row)]
 
     loads[4].wait()
-    for ch in range(nch - 1):
+    for ch in range(nch - 2):
         more = project(ch, c_cp[ch])
         total = more if total is None else total + more
     for d in range(1, n_row):
@@ -251,8 +256,9 @@
         src = pl.ds(pl.multiple_of(base + ((me_r + n_row - d) % n_row) * piece, piece), piece)
         wf_cp.append(send(gw.at[src], gw.at[src], wf_s.at[d], wf_r.at[d], sib_id))
     gw_ref[mine] = gw[mine]
-    more = project(nch - 1, c_cp[nch - 1])
-    total = more if total is None else total + more
+    for ch in range(nch - 2, nch):
+        more = project(ch, c_cp[ch])
+        total = more if total is None else total + more
     gi_ref[...] = total.astype(BF)
     bias = bsend[...]
     for d in range(1, n_row):
@@ -273,7 +279,7 @@
     rows, feat = grad_out.shape
     cap, blk = adj_blocks.shape[2], adj_blocks.shape[-1]
     group = max(d for d in range(1, 17) if cap % d == 0)
-    nch = 2
+    nch = 4
     fc = feat // nch
     n_z = n_col // 2
     piece = feat // 2 // n_row

time: 34.5 us -> 35 us (1.014)
  Pallas kernels: 30.7 us -> 31.2 us
    pallas_call x1, Pallas kernels: 30.7 us -> 31.2 us  [body(): pl.pallas_call(functools.partial(kernel, (n_row, n_col, nch, cap, group,...]
where the time goes in v1:
time: 35 us; the launch traced here: 34.9 us
  Pallas kernels  31.2 us (89%)
  other arithmetic  1.69 us (5%)
  between operations  1.32 us (4%)
  local copies, waits for them, and re-layouts  0.66 us (2%)
    pallas_call x1, Pallas kernels, body(): pl.pallas_call(functools.partial(kernel, (n_row, n_col, nch, cap, group,...  31.2 us
    mul x1, other arithmetic, body(): gw.astype(F32) * factor  1.11 us

profile of v1, /device:TPU:0, one launch (start us, length us, event | category | flops | bytes accessed | tf_op | source)
XLA Modules:
  0.0 34.9 jit_solution(8349435109830886848)
XLA Ops:
  0.6 0.0 copy-start
  1.3 0.0 copy-done
  1.3 31.2 %shard_map.94 = (bf16[128,512]{1,0:T(8,128)(2,1)S(1)}, bf16[512,512]{1,0:T(8,128)(2,1)S(1)}, f32[8,128]{1,0:T(8,128)S(1)}) custom-call(bf16[128,512]{1,0:T(8,128)(2,1)} %go_ref.1, s32[128,512]{1,0:T(8,128)} %mask_ref.1, bf16[128,512]{1,0:T(8,128)(2,1)} %agg_ref.1, bf16[512,512]{1,0:T(8,128)(2,1)} %w_ref.1, bf16[1,1,5,128,128]{4,3,2,1,0:T(8,128)(2,1)} %blk_ref.1, ...), custom_call_target="tpu_custom_call" | custom-call | tf_op jit(solution)/shard_map/pallas_call | solution.py:322
  32.5 0.6 %multiply_bitcast_fusion = f32[512]{0:T(512)} fusion(f32[8,128]{1,0:T(8,128)S(1)} %get-tuple-element.8), kind=kLoop, calls=%fused_computation.1 | loop fusion | flops 512 | bytes 4096 | tf_op jit(solution)/shard_map/mul | solution.py:335
  33.1 1.1 %convert_multiply_fusion = f32[512,512]{1,0:T(8,128)} fusion(bf16[512,512]{1,0:T(8,128)(2,1)S(1)} %get-tuple-element.7), kind=kLoop, calls=%fused_computation | loop fusion | flops 524288 | bytes 1572864 | tf_op jit(solution)/shard_map/mul | solution.py:335
  34.2 0.7 %copy.12 = bf16[1,128,512]{2,1,0:T(8,128)(2,1)} copy(bf16[1,128,512]{2,1,0:T(8,128)(2,1)S(1)} %bitcast.3) | data formatting | bytes 262144
Async XLA Ops:
  0.6 0.7 %copy-start = (s32[1,1,5]{2,1,0:T(1,128)S(1)}, s32[1,1,5]{2,1,0:T(1,128)}, u32[]{:S(2)}) copy-start(s32[1,1,5]{2,1,0:T(1,128)} %pos_ref.1) | copy-start | bytes 64

commit v2 on v1

--- a/solution.py
+++ b/solution.py
@@ -23,9 +23,9 @@
     n_row, n_col, nch, cap, group, scatter = cfg
     n_z = n_col // 2
     gath = scr[:nch]
-    lhs, cbuf, rbuf, asib, gpart, grecv, zsend, zrecv, gw, go_v, mask_v, agg_v, w_v, blk_v, bsend, brecv = scr[nch:nch + 16]
+    lhs, cbuf, rbuf, asib, gpart, grecv, zsend, zrecv, gw, go_v, mask_v, agg_v, w_v, blk_v, bsend, brecv, w_t = scr[nch:nch + 17]
     (ag_s, ag_r, fw_s, fw_r, c_s, c_r, as_s, as_r, g_s, g_r, z_s, z_r, wz_s, wz_r, wr_s, wr_r, wf_s, wf_r,
-     b_s, b_r, in_s, sb_s, sb_r) = scr[nch + 16:]
+     b_s, b_r, in_s, sb_s, sb_r) = scr[nch + 17:]
     rows, feat = go_ref.shape
     fc = feat // nch
     blk = blk_ref.shape[-1]
@@ -94,8 +94,7 @@
             send_when(has_next[way], lambda way=way: copy(
                 own, own, ag_s.at[ch, way, 0], ag_r.at[ch, way, 0], next_id[way]))
 
-    for ch in range(2):
-        depart(ch)
+    depart(0)
 
     loads[2].wait()
     agg_cp.wait_recv()
@@ -168,11 +167,6 @@
             cbuf[ch] = acc_ref[...].astype(BF).reshape(n_row, rows, fc)
         cps = [send(cbuf.at[ch, (me_r + d) % n_row], rbuf.at[ch, d - 1], c_s.at[ch, d - 1], c_r.at[ch, d - 1], row_id(d))
                for d in range(1, n_row)]
-        sums = lax.dot_general(ones, gath[ch][...].reshape(n_col * rows, fc), (((1,), (0,)), ((), ())),
-                               preferred_element_type=F32)
-        for i in range(fc // lanes):
-            at = ch * (fc // lanes) + i
-            bsend[at:at + 1, :] = sums[0:1, i * lanes:(i + 1) * lanes]
         return cps
 
     total = None
@@ -183,8 +177,11 @@
         s = cbuf[ch, me_r].astype(F32)
         for d in range(1, n_row):
             s += rbuf[ch, d - 1].astype(F32)
-        return lax.dot_general(s.astype(BF), w_v[:, ch * fc:(ch + 1) * fc], (((1,), (1,)), ((), ())),
-                               preferred_element_type=F32)
+        return jnp.dot(s.astype(BF), w_t[ch * fc:(ch + 1) * fc], preferred_element_type=F32)
+
+    def turn_weight():
+        loads[4].wait()
+        w_t[...] = w_v[...].T
 
     base = core * half
     at_row = pl.ds(pl.multiple_of(base + me_r * piece, piece), piece)
@@ -235,20 +232,25 @@
     c_cp = []
     todo = []
     for ch in range(nch):
-        at = 1.9 * (ch // 2) + 0.1 * ch
-        if ch >= 2:
-            todo.append((at - 1.6 + 0.8 * (ch % 2), functools.partial(depart, ch)))
+        at = 1.9 * ch
+        if ch >= 1:
+            todo.append((at - 1.4, functools.partial(depart, ch)))
         for step in range(n_z - 1):
             todo.append((at + step, functools.partial(relay, ch, step)))
         todo.append((at + n_z - 2 + 0.85, lambda ch=ch: c_cp.append(contribute(ch))))
-    todo += [(0.7, spread), (1.6, row_sum), (n_z - 0.91, z_sum), (n_z + 0.6, row_gather)]
+    todo += [(0.7, spread), (1.6, row_sum), (n_z - 1.5, z_sum), (n_z - 1.05, turn_weight), (n_z - 0.5, row_gather)]
     for _, act in sorted(todo, key=lambda item: item[0]):
         act()
 
+    for ch in range(nch):
+        sums = lax.dot_general(ones, gath[ch][...].reshape(n_col * rows, fc), (((1,), (0,)), ((), ())),
+                               preferred_element_type=F32)
+        for i in range(fc // lanes):
+            at = ch * (fc // lanes) + i
+            bsend[at:at + 1, :] = sums[0:1, i * lanes:(i + 1) * lanes]
     b_cp = [send(bsend, brecv.at[d - 1], b_s.at[d - 1], b_r.at[d - 1], row_id(d)) for d in range(1, n_row)]
 
-    loads[4].wait()
-    for ch in range(nch - 2):
+    for ch in range(nch - 1):
         more = project(ch, c_cp[ch])
         total = more if total is None else total + more
     for d in range(1, n_row):
@@ -256,7 +258,7 @@
         src = pl.ds(pl.multiple_of(base + ((me_r + n_row - d) % n_row) * piece, piece), piece)
         wf_cp.append(send(gw.at[src], gw.at[src], wf_s.at[d], wf_r.at[d], sib_id))
     gw_ref[mine] = gw[mine]
-    for ch in range(nch - 2, nch):
+    for ch in range(nch - 1, nch):
         more = project(ch, c_cp[ch])
         total = more if total is None else total + more
     gi_ref[...] = total.astype(BF)
@@ -279,7 +281,7 @@
     rows, feat = grad_out.shape
     cap, blk = adj_blocks.shape[2], adj_blocks.shape[-1]
     group = max(d for d in range(1, 17) if cap % d == 0)
-    nch = 4
+    nch = 2
     fc = feat // nch
     n_z = n_col // 2
     piece = feat // 2 // n_row
@@ -309,6 +311,7 @@
         pltpu.VMEM((cap, blk, blk), BF),
         pltpu.VMEM((brows, 128), F32),
         pltpu.VMEM((n_row - 1, brows, 128), F32),
+        pltpu.VMEM((feat, feat), BF),
     ]
     sems = [dma((nch, 2, n_z - 1)), dma((nch, 2, n_z - 1)), dma((nch, 2, n_z - 1)), dma((nch, 2, n_z - 1)),
             dma((nch, n_row - 1)), dma((nch, n_row - 1)), dma(()), dma(()),

time: 35 us -> 34.1 us (0.974)
  Pallas kernels: 31.2 us -> 30.3 us
    pallas_call x1, Pallas kernels: 31.2 us -> 30.3 us  [body(): pl.pallas_call(functools.partial(kernel, (n_row, n_col, nch, cap, group,...]
where the time goes in v2:
time: 34.1 us; the launch traced here: 34 us
  Pallas kernels  30.3 us (89%)
  other arithmetic  1.69 us (5%)
  between operations  1.32 us (4%)
  local copies, waits for them, and re-layouts  0.66 us (2%)
    pallas_call x1, Pallas kernels, body(): pl.pallas_call(functools.partial(kernel, (n_row, n_col, nch, cap, group,...  30.3 us
    mul x1, other arithmetic, body(): gw.astype(F32) * factor  1.11 us

profile of v2, /device:TPU:0, one launch (start us, length us, event | category | flops | bytes accessed | tf_op | source)
XLA Modules:
  0.0 34.0 jit_solution(8904656466776365957)
XLA Ops:
  0.6 0.0 copy-start
  1.3 0.0 copy-done
  1.3 30.3 %shard_map.94 = (bf16[128,512]{1,0:T(8,128)(2,1)S(1)}, bf16[512,512]{1,0:T(8,128)(2,1)S(1)}, f32[8,128]{1,0:T(8,128)S(1)}) custom-call(bf16[128,512]{1,0:T(8,128)(2,1)} %go_ref.1, s32[128,512]{1,0:T(8,128)} %mask_ref.1, bf16[128,512]{1,0:T(8,128)(2,1)} %agg_ref.1, bf16[512,512]{1,0:T(8,128)(2,1)} %w_ref.1, bf16[1,1,5,128,128]{4,3,2,1,0:T(8,128)(2,1)} %blk_ref.1, ...), custom_call_target="tpu_custom_call" | custom-call | tf_op jit(solution)/shard_map/pallas_call | solution.py:325
  31.6 0.6 %multiply_bitcast_fusion = f32[512]{0:T(512)} fusion(f32[8,128]{1,0:T(8,128)S(1)} %get-tuple-element.8), kind=kLoop, calls=%fused_computation.1 | loop fusion | flops 512 | bytes 4096 | tf_op jit(solution)/shard_map/mul | solution.py:338
  32.2 1.1 %convert_multiply_fusion = f32[512,512]{1,0:T(8,128)} fusion(bf16[512,512]{1,0:T(8,128)(2,1)S(1)} %get-tuple-element.7), kind=kLoop, calls=%fused_computation | loop fusion | flops 524288 | bytes 1572864 | tf_op jit(solution)/shard_map/mul | solution.py:338
  33.3 0.7 %copy.12 = bf16[1,128,512]{2,1,0:T(8,128)(2,1)} copy(bf16[1,128,512]{2,1,0:T(8,128)(2,1)S(1)} %bitcast.3) | data formatting | bytes 262144
Async XLA Ops:
  0.6 0.7 %copy-start = (s32[1,1,5]{2,1,0:T(1,128)S(1)}, s32[1,1,5]{2,1,0:T(1,128)}, u32[]{:S(2)}) copy-start(s32[1,1,5]{2,1,0:T(1,128)} %pos_ref.1) | copy-start | bytes 64

commit v3 on v2

--- a/solution.py
+++ b/solution.py
@@ -229,6 +229,13 @@
             wr_cp.append(send(gw.at[at_row], gw.at[at_row], wr_s.at[d - 1], wr_r.at[d - 1], row_id(d)))
         wf_cp.append(send(gw.at[at_row], gw.at[at_row], wf_s.at[0], wf_r.at[0], sib_id))
 
+    def bias_sum(ch):
+        sums = lax.dot_general(ones, gath[ch][...].reshape(n_col * rows, fc), (((1,), (0,)), ((), ())),
+                               preferred_element_type=F32)
+        for i in range(fc // lanes):
+            at = ch * (fc // lanes) + i
+            bsend[at:at + 1, :] = sums[0:1, i * lanes:(i + 1) * lanes]
+
     c_cp = []
     todo = []
     for ch in range(nch):
@@ -238,16 +245,11 @@
         for step in range(n_z - 1):
             todo.append((at + step, functools.partial(relay, ch, step)))
         todo.append((at + n_z - 2 + 0.85, lambda ch=ch: c_cp.append(contribute(ch))))
+        todo.append((at + n_z - 2 + 0.87, functools.partial(bias_sum, ch)))
     todo += [(0.7, spread), (1.6, row_sum), (n_z - 1.5, z_sum), (n_z - 1.05, turn_weight), (n_z - 0.5, row_gather)]
     for _, act in sorted(todo, key=lambda item: item[0]):
         act()
 
-    for ch in range(nch):
-        sums = lax.dot_general(ones, gath[ch][...].reshape(n_col * rows, fc), (((1,), (0,)), ((), ())),
-                               preferred_element_type=F32)
-        for i in range(fc // lanes):
-            at = ch * (fc // lanes) + i
-            bsend[at:at + 1, :] = sums[0:1, i * lanes:(i + 1) * lanes]
     b_cp = [send(bsend, brecv.at[d - 1], b_s.at[d - 1], b_r.at[d - 1], row_id(d)) for d in range(1, n_row)]
 
     for ch in range(nch - 1):

time: 34.1 us -> 34.1 us (level)
  no operation moved by 1% of the time
where the time goes in v3:
time: 34.1 us; the launch traced here: 34 us
  Pallas kernels  30.3 us (89%)
  other arithmetic  1.69 us (5%)
  between operations  1.32 us (4%)
  local copies, waits for them, and re-layouts  0.66 us (2%)
    pallas_call x1, Pallas kernels, body(): pl.pallas_call(functools.partial(kernel, (n_row, n_col, nch, cap, group,...  30.3 us
    mul x1, other arithmetic, body(): gw.astype(F32) * factor  1.11 us

profile of v3, /device:TPU:0, one launch (start us, length us, event | category | flops | bytes accessed | tf_op | source)
XLA Modules:
  0.0 34.0 jit_solution(16181215093132202140)
XLA Ops:
  0.6 0.0 copy-start
  1.3 0.0 copy-done
  1.3 30.3 %shard_map.94 = (bf16[128,512]{1,0:T(8,128)(2,1)S(1)}, bf16[512,512]{1,0:T(8,128)(2,1)S(1)}, f32[8,128]{1,0:T(8,128)S(1)}) custom-call(bf16[128,512]{1,0:T(8,128)(2,1)} %go_ref.1, s32[128,512]{1,0:T(8,128)} %mask_ref.1, bf16[128,512]{1,0:T(8,128)(2,1)} %agg_ref.1, bf16[512,512]{1,0:T(8,128)(2,1)} %w_ref.1, bf16[1,1,5,128,128]{4,3,2,1,0:T(8,128)(2,1)} %blk_ref.1, ...), custom_call_target="tpu_custom_call" | custom-call | tf_op jit(solution)/shard_map/pallas_call | solution.py:327
  31.6 0.6 %multiply_bitcast_fusion = f32[512]{0:T(512)} fusion(f32[8,128]{1,0:T(8,128)S(1)} %get-tuple-element.8), kind=kLoop, calls=%fused_computation.1 | loop fusion | flops 512 | bytes 4096 | tf_op jit(solution)/shard_map/mul | solution.py:340
  32.2 1.1 %convert_multiply_fusion = f32[512,512]{1,0:T(8,128)} fusion(bf16[512,512]{1,0:T(8,128)(2,1)S(1)} %get-tuple-element.7), kind=kLoop, calls=%fused_computation | loop fusion | flops 524288 | bytes 1572864 | tf_op jit(solution)/shard_map/mul | solution.py:340
  33.3 0.7 %copy.12 = bf16[1,128,512]{2,1,0:T(8,128)(2,1)} copy(bf16[1,128,512]{2,1,0:T(8,128)(2,1)S(1)} %bitcast.3) | data formatting | bytes 262144
Async XLA Ops:
  0.6 0.7 %copy-start = (s32[1,1,5]{2,1,0:T(1,128)S(1)}, s32[1,1,5]{2,1,0:T(1,128)}, u32[]{:S(2)}) copy-start(s32[1,1,5]{2,1,0:T(1,128)} %pos_ref.1) | copy-start | bytes 64
